TPU v7x, 32 devices: a whole 2x2x4 slice. The times are simulated.
32 devices in a mesh: section: 2 (over x), dp: 16 (over z, y, core).
Axes of the slice: x: 2, y: 2, z: 4, core: 2. Of those that a mesh axis runs over, the one named last changes fastest.
Arguments:
- hidden_in: bfloat16 [2, 16, 512, 768], P(None, 'dp'), may hold values from -6 to 6
- seg_ids: int32 [2, 16, 512], P(None, 'dp'), may hold values from 0 to 3, never falling along the last dimension, each value on 1 to 256 neighbouring positions
- pair_ids: int32 [2, 64], P(None, 'dp'), may hold values from 0 to 63, as said below
- w_qkv: bfloat16 [2, 768, 2304], P('section'), may hold values from -0.21875 to 0.21875
- b_query: bfloat16 [2, 768], P('section'), may hold values from -3 to 3
- b_value: bfloat16 [2, 768], P('section'), may hold values from -3 to 3
- w_attn_out: bfloat16 [2, 768, 768], P('section'), may hold values from -0.875 to 0.875
- b_attn_out: bfloat16 [2, 768], P('section'), may hold values from -1.75 to 1.75
- ln1_gain: bfloat16 [2, 768], P('section'), may hold values from 0.5 to 1.5
- ln1_bias: bfloat16 [2, 768], P('section'), may hold values from -1.75 to 1.75
- w_in: bfloat16 [2, 768, 3072], P('section'), may hold values from -0.21875 to 0.21875
- b_in: bfloat16 [2, 3072], P('section'), may hold values from -3 to 3
- w_out: bfloat16 [2, 3072, 768], P('section'), may hold values from -0.109375 to 0.109375
- b_out: bfloat16 [2, 768], P('section'), may hold values from -1.75 to 1.75
- ln2_gain: bfloat16 [2, 768], P('section'), may hold values from 0.5 to 1.5
- ln2_bias: bfloat16 [2, 768], P('section'), may hold values from -0.625 to 0.625
Outputs:
- pooled: float32 [2, 64, 768], P(None, 'dp', 'section')
- seg_loss: float32 [2, 64], P(None, 'dp')
- grad_input: float32 [2, 16, 512, 768], P(None, 'dp', None, 'section')
- grad_w_qkv: float32 [2, 768, 2304], P('section', 'dp')
- grad_b_query: float32 [2, 768], P('section', 'dp')
- grad_b_value: float32 [2, 768], P('section', 'dp')
- grad_w_attn_out: float32 [2, 768, 768], P('section', 'dp')
- grad_b_attn_out: float32 [2, 768], P('section', 'dp')
- grad_ln1_gain: float32 [2, 768], P('section', 'dp')
- grad_ln1_bias: float32 [2, 768], P('section', 'dp')
- grad_w_in: float32 [2, 768, 3072], P('section', 'dp')
- grad_b_in: float32 [2, 3072], P('section', 'dp')
- grad_w_out: float32 [2, 3072, 768], P('section', 'dp')
- grad_b_out: float32 [2, 768], P('section', 'dp')
- grad_ln2_gain: float32 [2, 768], P('section', 'dp')
- grad_ln2_bias: float32 [2, 768], P('section', 'dp')
Inputs may be any that keep to these rules, and one draw needn't show every extreme that they name: `seg_ids`: in each row the document numbers never fall and all 4 of them occur. In each micro-batch pair_ids is a permutation of the 64 documents forming one cycle; no document is its own partner.
All inputs are finite; a program needn't handle non-finite values.
Results may differ from a plain program's by a relative error of at most 0.02.
Values may be sent and summed in bfloat16 or wider, within the bound.
A program may use at most 256 MiB of HBM per device.

v0:
```python
import functools
import jax, jax.numpy as jnp
from jax import lax
from jax.experimental import pallas as pl
from jax.experimental.pallas import tpu as pltpu
from jax.sharding import PartitionSpec as P

HEADS = 12
HEAD_DIM = 64
SEGS = 4
UNIT_EPS = 1e-06
TEMPER = 20.0
MASK_FILL = 1000000000.0
NORM_EPS = 1e-12
BF = jnp.bfloat16
F32 = jnp.float32
VMEM_LIMIT = 60 * 2**20
MESH = pl.DeviceIdType.MESH
ANY = pl.BlockSpec(memory_space=pl.ANY)
VM = pl.BlockSpec(memory_space=pltpu.VMEM)


def dot(a, b):
    return jnp.dot(a, b, preferred_element_type=F32)


def dot_nt(a, b):
    return lax.dot_general(a, b, (((1,), (1,)), ((), ())), preferred_element_type=F32)


def dot_tn(a, b):
    return lax.dot_general(a, b, (((0,), (0,)), ((), ())), preferred_element_type=F32)


def split3(v):
    hi = v.astype(BF)
    rest = v - hi.astype(F32)
    mid = rest.astype(BF)
    low = (rest - mid.astype(F32)).astype(BF)
    return hi, mid, low


def members(seg_row):
    rows = lax.broadcasted_iota(jnp.int32, (16, seg_row.shape[1]), 0)
    return jnp.where(rows == seg_row, 1.0, 0.0).astype(BF)


def normed_rows(rows):
    centre = rows - jnp.mean(rows, axis=-1, keepdims=True)
    scale = lax.rsqrt(jnp.mean(centre * centre, axis=-1, keepdims=True) + NORM_EPS)
    return centre * scale, scale


def gelu_pair(u):
    mag = jnp.abs(u)
    t = 1.0 / (1.0 + (0.3275911 * 0.7071067811865476) * mag)
    e = jnp.exp(-0.5 * (u * u))
    poly = t * (0.127414796 + t * (-0.142248368 + t * (0.7107068705 + t * (-0.7265760135 + t * 0.5307027145))))
    tail = poly * e
    cdf = jnp.where(u >= 0.0, 1.0 - tail, tail)
    return u * cdf, cdf + (u * 0.3989422804014327) * e


def codes(mem):
    lanes = lax.rem(lax.broadcasted_iota(jnp.int32, (16, 128), 1), HEAD_DIM)
    pick = jnp.where(lanes == lax.broadcasted_iota(jnp.int32, (16, 128), 0), 1.0, 0.0)
    pick = jnp.where(lanes < SEGS, pick, 0.0).astype(BF)
    key_code = dot_tn(mem, pick)
    active = jnp.where(lanes[:1] < SEGS, 1.0, 0.0)
    return key_code.astype(BF), ((key_code - active) * MASK_FILL).astype(BF)


def documents(mem, pool):
    counts = jnp.maximum(jnp.sum(mem.astype(F32), axis=1, keepdims=True)[:8], 1.0)
    pooled = pool[:8, :] / counts
    radius = lax.rsqrt(jnp.sum(pooled * pooled, axis=-1, keepdims=True) + UNIT_EPS)
    return pooled, radius, counts


def message(unit, pairs):
    half = unit.shape[1] // 2
    tag = [jnp.broadcast_to(pairs[:, j:j + 1].astype(F32), (1, 128)) for j in range(SEGS)]
    tag = jnp.concatenate(tag + [jnp.zeros((8 - SEGS, 128), F32)], axis=0)
    return jnp.concatenate([jnp.concatenate([unit[:, :half], tag], axis=1), jnp.concatenate([unit[:, half:], tag], axis=1)], axis=0).astype(BF)


def fwd_kernel(tb, fc, peers,
    x_h, seg, pairs, wqkv_h, bq, bv, wat_h, bat, g1, b1, win_h, bin_, wout_h, bout, g2, b2,
    pool_o, x_o, qkv_h, lse_o, c_h, z1_h, s12_o, hb_h, gp_h, act_h, z2_h, msgs_o,
    x_s, wqkv, wat, win, wout, qkv, c_s, hb_s, z1_s, gp_s, act_s, z2_s, y_s, yf, msgs, kcode, qcode,
    insem, wsem, outsem, send_sem, recv_sem, msg_send, msg_recv):
    sec = lax.axis_index("section")
    me = lax.axis_index("dp")
    other = {"section": 1 - sec}
    M, T, D = x_s.shape
    FF = win.shape[1]
    nb = T // tb

    ws = [pltpu.make_async_copy(a, b, wsem.at[i]) for i, (a, b) in enumerate(
        ((wqkv_h, wqkv), (wat_h, wat), (win_h, win), (wout_h, wout)))]
    barrier = pltpu.get_barrier_semaphore()

    @pl.when(sec == 0)
    def _():
        pltpu.make_async_copy(x_h.at[0], x_s.at[0], insem.at[0]).start()
    ws[0].start()
    pl.semaphore_signal(barrier, inc=1, device_id=other, device_id_type=MESH)
    for d in range(1, peers):
        pl.semaphore_signal(barrier, inc=1, device_id={"dp": lax.rem(me + d, peers)}, device_id_type=MESH)
    for w in ws[1:]:
        w.start()

    @pl.when(sec == 0)
    def _():
        for m in range(1, M):
            pltpu.make_async_copy(x_h.at[m], x_s.at[m], insem.at[m]).start()

    lane = lax.broadcasted_iota(jnp.int32, (1, 128), 1)
    low_half = lane < HEAD_DIM

    def block(start):
        return pl.ds(start if isinstance(start, int) else pl.multiple_of(start, tb), tb)

    def out_copies(m, i):
        r = block(i * tb)
        span = block(m * T + i * tb)
        pairs = [(a.at[m, r], b.at[m, r]) for a, b in ((c_s, c_h), (hb_s, hb_h), (z1_s, z1_h), (z2_s, z2_h), (gp_s, gp_h))]
        pairs += [(act_s.at[m, r, j * D:(j + 1) * D], act_h.at[j, span]) for j in range(FF // D)]
        return [pltpu.make_async_copy(a, b, outsem.at[m, i, j]) for j, (a, b) in enumerate(pairs)]

    def whole_copies(m):
        return [pltpu.make_async_copy(a.at[m], b.at[m], outsem.at[m, nb, j]) for j, (a, b) in enumerate(((x_s, x_o), (qkv, qkv_h)))]

    def handoff(m, i):
        r = block(i * tb)
        return pltpu.make_async_remote_copy(src_ref=y_s.at[m, r], dst_ref=x_s.at[m, r], send_sem=send_sem.at[m, i],
            recv_sem=recv_sem.at[m, i], device_id=other, device_id_type=MESH)

    def msg_copy(d):
        return pltpu.make_async_remote_copy(src_ref=msgs.at[me], dst_ref=msgs.at[me], send_sem=msg_send.at[d - 1], recv_sem=msg_recv.at[d - 1],
            device_id={"dp": lax.rem(me + d, peers)}, device_id_type=MESH)

    def micro_step(m, _):
        mem = members(seg[m])
        kcode[...], qcode[...] = codes(mem)

        @pl.when(sec == 0)
        def _():
            pltpu.make_async_copy(x_h.at[m], x_s.at[m], insem.at[m]).wait()

        @pl.when(m == 0)
        def _():
            ws[0].wait()

        @pl.when(sec != 0)
        def _():
            for i in range(nb):
                handoff(m, i).wait_recv()
        xi = x_s[m]
        for j, b in ((0, bq), (1, None), (2, bv)):
            cols = slice(j * D, (j + 1) * D)
            v = dot(xi, wqkv[:, cols])
            if b is not None:
                v = v + b[...].astype(F32)
            qkv[m, :, cols] = v.astype(BF)
        for cp in whole_copies(m):
            cp.start()
        ones = jnp.ones((T, 128), BF)
        def block_step(i, _):
            r = block(i * tb)
            key_code = kcode[...]
            qc = qcode[r, :]
            lses = jnp.zeros((tb, 128), F32)
            for p in range(HEADS // 2):
                cols = slice(p * 128, (p + 1) * 128)
                k2 = qkv[m, :, D + p * 128:D + (p + 1) * 128]
                v2 = jnp.concatenate([qkv[m, :, 2 * D + p * 128:2 * D + (p + 1) * 128], ones], axis=1)
                q2 = qkv[m, r, cols] * (HEAD_DIM ** -0.5)
                halves = []
                for h in range(2):
                    if h == 0:
                        s = dot_nt(jnp.where(low_half, q2, qc), jnp.where(low_half, k2, key_code))
                    else:
                        s = dot_nt(jnp.where(low_half, qc, q2), jnp.where(low_half, key_code, k2))
                    mx = jnp.max(s, axis=-1, keepdims=True)
                    e = jnp.exp(s - mx).astype(BF)
                    c = dot(e, v2)
                    l = c[:, 128:]
                    halves.append(c[:, :128] / l)
                    lses = jnp.where(lane == 2 * p + h, mx + jnp.log(l), lses)
                c_s[m, r, cols] = jnp.where(low_half, halves[0], halves[1]).astype(BF)
            lse_o[m, :, r] = jnp.transpose(lses)[:16, :]

            @pl.when(jnp.logical_and(m == 0, i == 0))
            def _():
                for w in ws[1:]:
                    w.wait()
                pl.semaphore_wait(barrier, max(peers, 1))
            r1 = x_s[m, r, :].astype(F32) + dot(c_s[m, r, :], wat[...]) + bat[...].astype(F32)
            z, scale = normed_rows(r1)
            acc = z * g1[...].astype(F32) + b1[...].astype(F32)
            hi = acc.astype(BF)
            hb_s[m, r, :] = hi
            z1_s[m, r, :] = z.astype(BF)
            s12_o[m, r, 0:1] = scale
            acc = acc + bout[...].astype(F32)
            nj = FF // fc
            us = [dot(hi, win[:, :fc])]
            for j in range(nj):
                cols = slice(j * fc, (j + 1) * fc)
                if j + 1 < nj:
                    us.append(dot(hi, win[:, (j + 1) * fc:(j + 2) * fc]))
                f, gp = gelu_pair(us[j] + bin_[:, cols].astype(F32))
                f = f.astype(BF)
                act_s[m, r, cols] = f
                gp_s[m, r, cols] = gp.astype(BF)
                acc = acc + dot(f, wout[cols, :])
            z, scale = normed_rows(acc)
            y = z * g2[...].astype(F32) + b2[...].astype(F32)
            y_s[m, r, :] = y.astype(BF)

            @pl.when(sec == 0)
            def _():
                handoff(m, i).start()
            z2_s[m, r, :] = z.astype(BF)
            s12_o[m, r, 1:2] = scale
            yf[r, :] = y
            for cp in out_copies(m, i):
                cp.start()
            return 0
        lax.fori_loop(0, nb, block_step, 0)

        @pl.when(sec != 0)
        def _():
            hi, mid, low = split3(yf[...])
            pool = (dot(mem, hi) + dot(mem, mid)) + dot(mem, low)
            pool_o[m] = pool
            if peers:
                @pl.when(m == 0)
                def _():
                    pooled, radius, _ = documents(mem, pool)
                    msgs[me] = message(pooled * radius, pairs[0:1, :])
                    for d in range(1, peers):
                        msg_copy(d).start()
        return 0
    lax.fori_loop(0, M, micro_step, 0)

    @pl.when(sec == 0)
    def _():
        pool_o[...] = jnp.zeros_like(pool_o)
        msgs_o[...] = jnp.zeros_like(msgs_o)

    if peers:
        @pl.when(sec != 0)
        def _():
            for d in range(1, peers):
                msg_copy(d).wait()
            msgs_o[...] = msgs[...]
    for m in range(M):
        for cp in whole_copies(m):
            cp.wait()
        for i in range(nb):
            for cp in out_copies(m, i):
                cp.wait()

    @pl.when(sec == 0)
    def _():
        for m in range(M):
            for i in range(nb):
                handoff(m, i).wait_send()


def stack_fwd(x, seg, pairs, weights, peers, tb=256, fc=768):
    M, T, D = x.shape
    FF = weights[7].shape[1]
    sds = jax.ShapeDtypeStruct
    out_shape = (sds((M, 16, D), F32), sds((M, T, D), BF), sds((M, T, 3 * D), BF), sds((M, 16, T), F32), sds((M, T, D), BF),
        sds((M, T, D), BF), sds((M, T, 2), F32), sds((M, T, D), BF), sds((M, T, FF), BF), sds((FF // D, M * T, D), BF), sds((M, T, D), BF), sds((max(peers, 1), 16, D // 2 + 128), BF))
    out_specs = (VM, ANY, ANY, VM, ANY, ANY, VM, ANY, ANY, ANY, ANY, VM)
    V = pltpu.VMEM
    S = pltpu.SemaphoreType.DMA
    nb = T // tb
    scratch = [V((M, T, D), BF), V((D, 3 * D), BF), V((D, D), BF), V((D, FF), BF), V((FF, D), BF), V((M, T, 3 * D), BF),
        V((M, T, D), BF), V((M, T, D), BF), V((M, T, D), BF), V((M, T, FF), BF), V((M, T, FF), BF), V((M, T, D), BF), V((M, T, D), BF),
        V((T, D), F32), V((max(peers, 1), 16, D // 2 + 128), BF), V((T, 128), BF), V((T, 128), BF), S((M,)), S((4,)), S((M, nb + 1, 5 + FF // D)), S((M, nb)), S((M, nb)),
        S((max(peers, 2) - 1,)), S((max(peers, 2) - 1,))]
    in_specs = (ANY, VM, VM, ANY, VM, VM, ANY, VM, VM, VM, ANY, VM, ANY, VM, VM, VM)
    return pl.pallas_call(functools.partial(fwd_kernel, tb, fc, peers), out_shape=out_shape, in_specs=in_specs, out_specs=out_specs,
        scratch_shapes=scratch, compiler_params=pltpu.CompilerParams(vmem_limit_bytes=VMEM_LIMIT, collective_id=0, has_side_effects=True),
        name="stack_fwd")(x, seg, pairs, *weights)


def rowsum8(v):
    return jnp.sum(v.reshape(v.shape[0] // 8, 8, v.shape[1]), axis=0)


def bwd_kernel(tb, fc, kb,
    seg, dp, lse, s12, qkv_h, c_h, z1_h, gp_h, z2_h, wqkv_h, wat_h, g1, win_h, wout_h, g2,
    vec_o, dx_h, dxb_h, db2_h, du_h, db1_h, dqkv_h,
    dyr, wqkv, wat, win, wout, qkv, c_s, z1, gp, z2, bias, dy_s, dr1, dc, delta, du, db2, db1, dqkv, dx, dxb, vacc, bacc,
    insem, wsem, outsem, send_sem, recv_sem):
    sec = lax.axis_index("section")
    other = {"section": 1 - sec}
    M, T, D = c_s.shape
    FF = win.shape[1]
    nb = T // tb

    ws = [pltpu.make_async_copy(a, b, wsem.at[i]) for i, (a, b) in enumerate(
        ((wout_h, wout), (win_h, win), (wat_h, wat), (wqkv_h, wqkv)))]

    def in_copies(m):
        pairs = [(z2_h, z2), (gp_h, gp), (z1_h, z1), (c_h, c_s), (qkv_h, qkv)]
        return [pltpu.make_async_copy(a.at[m], b.at[m], insem.at[m, i]) for i, (a, b) in enumerate(pairs)]
    first = in_copies(0)
    first[0].start()
    ws[0].start()
    barrier = pltpu.get_barrier_semaphore()
    pl.semaphore_signal(barrier, inc=1, device_id=other, device_id_type=MESH)
    for a, b in zip(first[1:], ws[1:]):
        a.start()
        b.start()
    first[4].start()
    for m in range(1, M):
        for a in in_copies(m):
            a.start()
    vacc[...] = jnp.zeros_like(vacc)
    bacc[...] = jnp.zeros_like(bacc)
    pl.semaphore_wait(barrier, 1)

    lane = lax.broadcasted_iota(jnp.int32, (1, 128), 1)
    low_half = lane < HEAD_DIM
    indicator = jnp.where(lax.broadcasted_iota(jnp.int32, (16, D), 1) // HEAD_DIM == lax.broadcasted_iota(jnp.int32, (16, D), 0), 1.0, 0.0).astype(BF)

    def out_copies(m):
        pairs = [(db2, db2_h), (du, du_h), (db1, db1_h), (dqkv, dqkv_h), (dx, dx_h), (dxb, dxb_h)]
        return [pltpu.make_async_copy(a.at[m], b.at[m], outsem.at[m, i]) for i, (a, b) in enumerate(pairs)]

    def handoff(m, i):
        r = pl.ds(i * tb if isinstance(i, int) else pl.multiple_of(i * tb, tb), tb)
        return pltpu.make_async_remote_copy(src_ref=dxb.at[m, r], dst_ref=dyr.at[m, r], send_sem=send_sem.at[m, i],
            recv_sem=recv_sem.at[m, i], device_id=other, device_id_type=MESH)

    def norm_pull(z, scale, gain, dy):
        g = dy * gain
        return scale * (g - jnp.mean(g, axis=-1, keepdims=True) - z * jnp.mean(g * z, axis=-1, keepdims=True))

    def micro_step(m, _):
        ins = in_copies(m)
        outs = out_copies(m)
        mem = members(seg[pl.ds(m, 1), :])
        bias[...] = (dot_tn(mem, mem) - 1.0) * MASK_FILL
        dp3 = jnp.concatenate(split3(dp[m]), axis=0)

        @pl.when(sec == 0)
        def _():
            for i in range(nb):
                handoff(m, i).wait_recv()

        @pl.when(m == 0)
        def _():
            ws[0].wait()
            ws[1].wait()
            ws[2].wait()
        for a in ins[:4]:
            a.wait()

        def tok_step(i, _):
            r = pl.ds(pl.multiple_of(i * tb, tb), tb)

            @pl.when(sec == 0)
            def _():
                dy_s[...] = dyr[m, r, :].astype(F32)

            @pl.when(sec != 0)
            def _():
                blk = members(seg[pl.ds(m, 1), r])
                dy_s[...] = dot_tn(jnp.concatenate([blk, blk, blk], axis=0), dp3)
            dy = dy_s[...]
            z = z2[m, r, :].astype(F32)
            dr2 = norm_pull(z, s12[m, r, 1:2], g2[...].astype(F32), dy)
            vacc[0] += rowsum8(dy * z)
            vacc[1] += rowsum8(dy)
            d2 = dr2.astype(BF)
            db2[m, r, :] = d2
            vacc[2] += rowsum8(d2.astype(F32))
            dh = dr2
            nj = FF // fc
            dfs = [dot_nt(d2, wout[:fc, :])]
            for j in range(nj):
                cols = slice(j * fc, (j + 1) * fc)
                if j + 1 < nj:
                    dfs.append(dot_nt(d2, wout[(j + 1) * fc:(j + 2) * fc, :]))
                dub = (dfs[j] * gp[m, r, cols].astype(F32)).astype(BF)
                du[m, r, cols] = dub
                bacc[:, cols] += rowsum8(dub.astype(F32))
                dh = dh + dot_nt(dub, win[:, cols])
            z = z1[m, r, :].astype(F32)
            d1 = norm_pull(z, s12[m, r, 0:1], g1[...].astype(F32), dh)
            vacc[3] += rowsum8(dh * z)
            vacc[4] += rowsum8(dh)
            dr1[r, :] = d1
            d1 = d1.astype(BF)
            db1[m, r, :] = d1
            vacc[5] += rowsum8(d1.astype(F32))
            dcb = dot_nt(d1, wat[...]).astype(BF)
            dc[r, :] = dcb
            prod = dcb.astype(F32) * c_s[m, r, :].astype(F32)
            hi = prod.astype(BF)
            low = (prod - hi.astype(F32)).astype(BF)
            delta[:, r] = dot_nt(indicator, hi) + dot_nt(indicator, low)
            return 0
        lax.fori_loop(0, nb, tok_step, 0)
        for o in outs[:3]:
            o.start()
        ins[4].wait()

        def att_step(p, _):
            cols = pl.ds(pl.multiple_of(p * 128, 128), 128)
            kcols = pl.ds(pl.multiple_of(p * 128 + D, 128), 128)
            vcols = pl.ds(pl.multiple_of(p * 128 + 2 * D, 128), 128)
            q2 = qkv[m, :, cols] * (HEAD_DIM ** -0.5)
            dc2 = dc[:, cols]
            dqt = jnp.zeros((128, T), F32)
            for i in range(T // kb):
                rows = slice(i * kb, (i + 1) * kb)
                k2 = qkv[m, rows, kcols]
                v2 = qkv[m, rows, vcols]
                dks, dvs = [], []
                for h in range(2):
                    pick = low_half if h == 0 else jnp.logical_not(low_half)
                    kh = jnp.where(pick, k2, 0)
                    vh = jnp.where(pick, v2, 0)
                    st = dot_nt(kh, q2) + bias[rows, :]
                    pt = jnp.exp(st - lse[m, pl.ds(2 * p + h, 1), :])
                    dpt = dot_nt(vh, dc2)
                    da = (pt * (dpt - delta[pl.ds(2 * p + h, 1), :])).astype(BF)
                    dvs.append(dot(pt.astype(BF), dc2))
                    dks.append(dot(da, q2))
                    dqt = dqt + dot_tn(kh, da)
                dqkv[m, rows, kcols] = jnp.where(low_half, dks[0], dks[1]).astype(BF)
                dqkv[m, rows, vcols] = jnp.where(low_half, dvs[0], dvs[1]).astype(BF)
            dqkv[m, :, cols] = (jnp.transpose(dqt) * (HEAD_DIM ** -0.5)).astype(BF)
            return 0
        lax.fori_loop(0, HEADS // 2, att_step, 0)
        outs[3].start()

        @pl.when(m == 0)
        def _():
            ws[3].wait()

        def dx_step(i, _):
            r = pl.ds(pl.multiple_of(i * tb, tb), tb)
            v = dr1[r, :] + dot_nt(dqkv[m, r, :], wqkv[...])
            dx[m, r, :] = v
            dxb[m, r, :] = v.astype(BF)
            vacc[6] += rowsum8(dqkv[m, r, :D].astype(F32))
            vacc[7] += rowsum8(dqkv[m, r, 2 * D:].astype(F32))

            @pl.when(sec != 0)
            def _():
                handoff(m, i).start()
            return 0
        lax.fori_loop(0, nb, dx_step, 0)
        outs[4].start()
        outs[5].start()
        return 0
    lax.fori_loop(0, M, micro_step, 0)
    vec_o[...] = jnp.concatenate([jnp.sum(vacc[...], axis=1)]
        + [jnp.sum(bacc[:, j * D:(j + 1) * D], axis=0, keepdims=True) for j in range(FF // D)] + [jnp.zeros((4, D), F32)], axis=0)
    for m in range(M):
        for o in out_copies(m):
            o.wait()

    @pl.when(sec != 0)
    def _():
        for m in range(M):
            for i in range(nb):
                handoff(m, i).wait_send()


def stack_bwd(seg, dp, stash, weights, tb=256, fc=768, kb=256):
    qkv, lse, c, z1, s12, gp, z2 = stash
    wqkv, bq, bv, wat, bat, g1, b1, win, bin_, wout, bout, g2, b2 = weights
    M, T, D = c.shape
    FF = win.shape[1]
    sds = jax.ShapeDtypeStruct
    out_shape = (sds((16, D), F32), sds((M, T, D), F32), sds((M, T, D), BF), sds((M, T, D), BF), sds((M, T, FF), BF), sds((M, T, D), BF), sds((M, T, 3 * D), BF))
    out_specs = (VM, ANY, ANY, ANY, ANY, ANY, ANY)
    V = pltpu.VMEM
    S = pltpu.SemaphoreType.DMA
    nb = T // tb
    scratch = [V((M, T, D), BF), V((D, 3 * D), BF), V((D, D), BF), V((D, FF), BF), V((FF, D), BF),
        V((M, T, 3 * D), BF), V((M, T, D), BF), V((M, T, D), BF), V((M, T, FF), BF), V((M, T, D), BF),
        V((T, T), F32), V((tb, D), F32), V((T, D), F32), V((T, D), BF), V((16, T), F32),
        V((M, T, FF), BF), V((M, T, D), BF), V((M, T, D), BF), V((M, T, 3 * D), BF), V((M, T, D), F32), V((M, T, D), BF),
        V((8, 8, D), F32), V((8, FF), F32), S((M, 5)), S((4,)), S((M, 6)), S((M, nb)), S((M, nb))]
    in_specs = (VM, VM, VM, VM, ANY, ANY, ANY, ANY, ANY, ANY, ANY, VM, ANY, ANY, VM)
    return pl.pallas_call(functools.partial(bwd_kernel, tb, fc, kb), out_shape=out_shape, in_specs=in_specs, out_specs=out_specs,
        scratch_shapes=scratch, compiler_params=pltpu.CompilerParams(vmem_limit_bytes=VMEM_LIMIT, collective_id=1, has_side_effects=True),
        name="stack_bwd")(seg, dp, lse, s12, qkv, c, z1, gp, z2, wqkv, wat, g1, win, wout, g2)


AFTER_TOKENS = (" ".join(("a2 a3 b0",)), " ".join(("b1",)))
AFTER_W = ("", " ".join(("a4 c0",)), " ".join(("a5 b2",)), " ".join(("a6 c1",)))
AFTER_A = " ".join(("b3",))
AFTER_PAIR = (" ".join(("a7",)), " ".join(("a8 c2",)), " ".join(("b4",)), "", " ".join(("c3",)), "")
BEFORE_Q = " ".join(("b5 b8",))
AFTER_Q = ("", " ".join(("v0 a9 c4 b6",)), "")
AT_THE_END = " ".join(("v1 a10 c5 d3", "b7 a11 c8 d4", "c6 b9 d5 c7", "v2 b10 d6 c9", "v3 d7 b11 c10", "d8 d9 c11 d10", "d11",))


def back_kernel(tb, xb, kb,
    seg, pool, pairs, msgs0, lse, s12, z2_h, gp_h, z1_h, c_h, qkv_h, hb_h, x_h, act_h, wout_h, win_h, wat_h, wqkv_h, g1, g2,
    vec_o, pooled_o, loss_o, g_qkv, g_at, g_in, g_out, dx_o, dxr_o,
    dyx, wqkv, wat, win, wout, qkv, c_s, z1, gp, z2, dr, dc, delta, db2, db1, vacc, bacc,
    msgs, dps, loss_w, dn_s, pooled_s, loss_s, pooled_r, loss_r, kcode, qcode, gathered, rhs, part, got_a, got_b, got_c, got_d, got_t, va, vb,
    insem, wsem, latesem, outsem, send_sem, recv_sem, msg_send, msg_recv, pool_sem, dx_sem,
    send_a, recv_a, send_b, recv_b, send_c, recv_c, send_d, recv_d):
    sec = lax.axis_index("section")
    me = lax.axis_index("dp")
    peers = msgs.shape[0]
    core = lax.rem(me, 2)
    y = lax.rem(lax.div(me, 2), 2)
    z = lax.div(me, 4)
    zlow = lax.rem(z, 2)
    zhigh = lax.div(z, 2)
    other = {"section": 1 - sec}
    sibling = {"dp": me + 1 - 2 * core}
    across = {"dp": me + 2 - 4 * y}
    near = {"dp": me + 4 - 8 * zlow}
    far = {"dp": me + 8 - 16 * zhigh}

    def remote(src, dst, ss, rs, target):
        return pltpu.make_async_remote_copy(src_ref=src, dst_ref=dst, send_sem=ss, recv_sem=rs, device_id=target, device_id_type=MESH)
    M, T, D = c_s.shape
    N = M * T
    FF = gp.shape[2]
    half = D // 2
    nb = T // tb
    nx = T // xb
    nj = FF // D
    chunks = got_a.shape[0]
    rows = got_a.shape[4]
    SL = 8
    zchunk = 2 * nj

    wcp = [pltpu.make_async_copy(a, b, wsem.at[i]) for i, (a, b) in enumerate(
        ((wout_h, wout), (win_h, win), (wat_h, wat), (wqkv_h, wqkv)))]

    def norm_copies(m):
        return [pltpu.make_async_copy(a.at[m], b, insem.at[m, i]) for i, (a, b) in enumerate(((z2_h, z2), (z1_h, z1)))]

    def in_copies(m):
        return [pltpu.make_async_copy(a.at[m], b.at[m], insem.at[m, 2 + i]) for i, (a, b) in enumerate(((gp_h, gp), (c_h, c_s), (qkv_h, qkv)))]

    def act_copy(t):
        return pltpu.make_async_copy(act_h.at[t], rhs.at[t % 2 if isinstance(t, int) else lax.rem(t, 2)], latesem.at[t])
    hb_copy = pltpu.make_async_copy(hb_h, rhs.at[0], latesem.at[nj])
    x_copy = pltpu.make_async_copy(x_h, rhs.at[1], latesem.at[nj + 1])
    norms = norm_copies(0)
    ins = in_copies(0)
    norms[0].start()
    wcp[0].start()
    barrier = pltpu.get_barrier_semaphore()
    pl.semaphore_signal(barrier, inc=1, device_id=other, device_id_type=MESH)
    for d in range(1, peers):
        pl.semaphore_signal(barrier, inc=1, device_id={"dp": lax.rem(me + d, peers)}, device_id_type=MESH)
    for a in [ins[0], wcp[1], norms[1], wcp[2], ins[1], ins[2], wcp[3]]:
        a.start()
    for m in range(1, M):
        for a in in_copies(m):
            a.start()
    act_copy(0).start()
    act_copy(1).start()
    vacc[...] = jnp.zeros_like(vacc)
    bacc[...] = jnp.zeros_like(bacc)

    def msg_copy(d):
        return remote(msgs.at[me], msgs.at[me], msg_send.at[d - 1], msg_recv.at[d - 1], {"dp": lax.rem(me + d, peers)})
    pool_copy = remote(pooled_s, pooled_r, pool_sem.at[0], pool_sem.at[1], other)
    loss_copy = remote(loss_s, loss_r, pool_sem.at[2], pool_sem.at[3], other)
    pl.semaphore_wait(barrier, peers)

    def head(m):
        eight = pl.ds(pl.multiple_of(m * SL, SL), SL)
        pooled, radius, counts = documents(members(seg[m]), pool[m])
        G = peers * SL
        lo = gathered[:, :SL, :half].astype(F32).reshape(G, half).astype(BF)
        hi = gathered[:, SL:, :half].astype(F32).reshape(G, half).astype(BF)
        partner = gathered[:, :SL, half:].astype(F32).reshape(G, 128)
        rid = lax.broadcasted_iota(jnp.int32, (G, G), 0)
        cid = lax.broadcasted_iota(jnp.int32, (G, G), 1)
        held = jnp.logical_and(lax.rem(rid, SL) < SEGS, lax.rem(cid, SL) < SEGS)
        logits = TEMPER * (dot_nt(lo, lo) + dot_nt(hi, hi))
        logits = jnp.where(jnp.logical_and(held, rid != cid), logits, -MASK_FILL)
        peak = jnp.max(logits, axis=-1, keepdims=True)
        exponent = jnp.exp(logits - peak)
        denom = jnp.sum(exponent, axis=-1, keepdims=True)
        doc = (lax.div(cid, SL) * SEGS + lax.rem(cid, SL)).astype(F32)
        target = jnp.where(jnp.logical_and(held, doc == partner[:, :1]), 1.0, 0.0)
        loss = peak + jnp.log(denom) - jnp.sum(target * logits, axis=-1, keepdims=True)
        dl = jnp.where(held, exponent / denom - target, 0.0).astype(BF)
        own = pl.ds(pl.multiple_of(me * SL, SL), SL)
        for side, part_of in ((0, lo), (1, hi)):
            dn_s[:, side * half:(side + 1) * half] = TEMPER * (dot(dl, part_of) + dot_tn(dl, part_of))
        dn = dn_s[own, :]
        loss_w[...] = jnp.broadcast_to(loss, (G, 128))
        loss_s[eight, :] = loss_w[own, :]
        dps[eight, :] = (radius * dn - radius * radius * radius * jnp.sum(pooled * dn, axis=-1, keepdims=True) * pooled) / counts

    @pl.when(sec != 0)
    def _():
        for m in range(M):
            pooled, radius, _ = documents(members(seg[m]), pool[m])
            pooled_s[m * SL:(m + 1) * SL, :] = pooled
            if m == 1:
                msgs[me] = message(pooled * radius, pairs[m:m + 1, :])
        for d in range(1, peers):
            msg_copy(d).start()
        pool_copy.start()

    lane = lax.broadcasted_iota(jnp.int32, (1, 128), 1)
    low_half = lane < HEAD_DIM
    indicator = jnp.where(lax.broadcasted_iota(jnp.int32, (16, D), 1) // HEAD_DIM == lax.broadcasted_iota(jnp.int32, (16, D), 0), 1.0, 0.0).astype(BF)

    def out_copy(m):
        return pltpu.make_async_copy(dyx.at[m], dx_o.at[m], outsem.at[m])

    def handoff(m, i):
        r = pl.ds(i * xb if isinstance(i, int) else pl.multiple_of(i * xb, xb), xb)
        return remote(dyx.at[m, r], dyx.at[m, r], send_sem.at[m, i], recv_sem.at[m, i], other)

    def dx_copy(m):
        return remote(dyx.at[m, :, half:], dxr_o.at[m], dx_sem.at[m, 0], dx_sem.at[m, 1], other)

    def norm_pull(zz, scale, gain, dy):
        g = dy * gain
        return scale * (g - jnp.mean(g, axis=-1, keepdims=True) - zz * jnp.mean(g * zz, axis=-1, keepdims=True))

    def slot(k):
        return k % 2 if isinstance(k, int) else lax.rem(k, 2)

    def copy_a(k):
        return remote(part.at[slot(k), :, :, :, 1 - core], got_a.at[k], send_a.at[k], recv_a.at[k], sibling)

    def copy_b(k):
        if not isinstance(k, int) or k != zchunk:
            return remote(got_a.at[k, :, :, 1 - y], got_b.at[k], send_b.at[k], recv_b.at[k], across)
        return remote(got_a.at[k, zhigh, zlow, 1 - y], got_d.at[k], send_b.at[k], recv_b.at[k], across)

    def copy_c(k):
        if k < nj:
            return remote(got_b.at[k], got_c.at[pl.ds(2 * (k // 2), 2)], send_c.at[k], recv_c.at[k], near)
        if k == zchunk:
            return remote(got_a.at[k, :, 1 - zlow], got_b.at[k], send_c.at[k], recv_c.at[k], near)
        return remote(got_b.at[k, :, 1 - zlow], got_c.at[k], send_c.at[k], recv_c.at[k], near)

    def copy_d(k):
        if not isinstance(k, int) or k < nj:
            return remote(got_b.at[k], got_t, send_d.at[k], recv_d.at[k], far)
        if k == zchunk:
            return remote(got_a.at[k, 1 - zhigh, zlow], got_c.at[k], send_d.at[k], recv_d.at[k], far)
        return remote(got_b.at[k, 1 - zhigh, zlow], got_d.at[k], send_d.at[k], recv_d.at[k], far)

    def e1(k):
        copy_a(k).wait_recv()

        for h in range(2):
            got_a[k, h] = got_a[k, h] + part[slot(k), h, :, :, core]
        if isinstance(k, int) and k == zchunk:
            copy_c(k).start()
        else:
            copy_b(k).start()
        copy_a(k).wait_send()

    def e2(k):
        if k == zchunk:
            copy_c(k).wait_recv()
            for h in range(2):
                got_a[k, h, zlow] = got_a[k, h, zlow] + got_b[k, h]
            copy_d(k).start()
            return
        copy_b(k).wait_recv()
        for h in range(2):
            got_b[k, h] = got_b[k, h] + got_a[k, h, :, y]
        if k < nj:
            @pl.when(zlow != k % 2)
            def _():
                copy_c(k).start()
        else:
            copy_c(k).start()

    def e3(k):
        if k < nj:
            @pl.when(zlow == k % 2)
            def _():
                copy_c(k).wait_recv()
                for h in range(2):
                    got_b[k, h] = got_b[k, h] + got_c[2 * (k // 2) + h]

                @pl.when(z != k)
                def _():
                    copy_d(k).start()
        elif k == zchunk:
            copy_d(k).wait_recv()
            got_a[k, zhigh, zlow] = got_a[k, zhigh, zlow] + got_c[k]
            copy_b(k).start()
        else:
            copy_c(k).wait_recv()
            for h in range(2):
                got_b[k, h, zlow] = got_b[k, h, zlow] + got_c[k, h]
            copy_d(k).start()

    def e4(k):
        if k == zchunk:
            copy_b(k).wait_recv()
            return got_a[k, zhigh, zlow, y].astype(F32) + got_d[k].astype(F32)
        copy_d(k).wait_recv()
        return got_b[k, zhigh, zlow].astype(F32) + got_d[k].astype(F32)

    def tile_out(k, lhs, right):
        def side(i, _):
            cols = pl.ds(pl.multiple_of(i * half, half), half)
            v = dot_tn(lhs[:, cols], right)
            part[slot(k), i] = v.astype(BF).reshape(part.shape[2:])
            return 0
        lax.fori_loop(0, 2, side, 0)
        copy_a(k).start()

    def products_t():
        def one(t, _):
            act_copy(t).wait()

            def side(i, _):
                cols = pl.ds(pl.multiple_of(i * half, half), half)
                v = dot_tn(rhs[lax.rem(t, 2), :, cols], db2[...].reshape(N, D)).astype(BF)
                for c in range(2):
                    for s in range(4):
                        part[slot(t), s // 2, s % 2, i, c] = v[(c * 4 + s) * rows:(c * 4 + s + 1) * rows]
                return 0
            lax.fori_loop(0, 2, side, 0)
            copy_a(t).start()

            @pl.when(t < nj - 2)
            def _():
                act_copy(t + 2).start()

            @pl.when(t == nj - 2)
            def _():
                hb_copy.start()

            @pl.when(t == nj - 1)
            def _():
                x_copy.start()

            @pl.when(jnp.logical_and(t >= 1, t <= 2))
            def _():
                e1(t - 1)
            return 0
        lax.fori_loop(0, nj, one, 0)

    def products_w():
        hb_copy.wait()

        def one(j, _):
            tile_out(nj + j, rhs.at[0], gp[:, :, pl.ds(pl.multiple_of(j * D, D), D)].reshape(N, D))
            for n, steps in enumerate(AFTER_W):
                if steps:
                    run_when(j == n, steps)
            return 0
        lax.fori_loop(0, nj, one, 0)

        def side(i, _):
            cols = pl.ds(pl.multiple_of(i * half, half), half)
            v = dot_tn(c_s[:, :, cols].reshape(N, half), db1[...].reshape(N, D))
            part[slot(2 * nj), i] = v.astype(BF).reshape(part.shape[2:])
            return 0
        lax.fori_loop(0, 2, side, 0)
        copy_a(2 * nj).start()
        for step in AFTER_A.split():
            run(step)

    def products_q():
        x_copy.wait()

        def one(j, _):
            tile_out(2 * nj + 1 + j, rhs.at[1], qkv[:, :, pl.ds(pl.multiple_of(j * D, D), D)].reshape(N, D))
            for n, steps in enumerate(AFTER_Q):
                if steps:
                    run_when(j == n, steps)
            return 0
        lax.fori_loop(0, 3, one, 0)

    def store(k):
        v = e4(k)
        if k < 2 * nj:
            g_in[:, (k - nj) * D:(k - nj + 1) * D] = v
        elif k == 2 * nj:
            g_at[...] = v
        else:
            g_qkv[:, (k - 2 * nj - 1) * D:(k - 2 * nj) * D] = v

    def store_w_out():
        copy_d(z).wait_recv()
        for s in range(4):
            g_out[s * rows:(s + 1) * rows, :] = got_b[z, s // 2, s % 2].astype(F32) + got_t[s // 2, s % 2].astype(F32)

    def run(step):
        what, k = step[0], int(step[1:])
        if what == "v":
            vec_step(k)
        elif what == "d":
            if k >= nj:
                store(k)
            elif k == nj - 1:
                store_w_out()
        else:
            {"a": e1, "b": e2, "c": e3}[what](k)

    def run_when(where, steps):
        @pl.when(where)
        def _():
            for step in steps.split():
                run(step)

    def one_pass(step, _):
        m = jnp.minimum(step, M - 1)
        norms = norm_copies(m)
        ins = in_copies(m)
        forming = jnp.logical_or(jnp.logical_and(step == M - 1, sec == 0), jnp.logical_and(step == M, sec != 0))
        behind = jnp.logical_and(step == M, sec != 0)

        @pl.when(step < M)
        def _():
            norm_pass(m, norms)

        @pl.when(forming)
        def _():
            products_t()

        @pl.when(step < M)
        def _():
            token_pass(m, norms, ins)

        @pl.when(forming)
        def _():
            run_when(behind, " ".join(AFTER_TOKENS))
            products_w()
            run_when(behind, " ".join(AFTER_PAIR))

        @pl.when(step < M)
        def _():
            attention_pass(m)
        return 0

    def norm_pass(m, norms):
        norms = norm_copies(m)
        ins = in_copies(m)
        mem = members(seg[m])
        kcode[...], qcode[...] = codes(mem)
        norms[0].wait()

        @pl.when(sec != 0)
        def _():
            @pl.when(m == 0)
            def _():
                gathered[...] = msgs0[...]

            @pl.when(m == 1)
            def _():
                for d in range(1, peers):
                    msg_copy(d).wait()
                gathered[...] = msgs[...]
            head(m)

            @pl.when(m == M - 1)
            def _():
                loss_copy.start()

        def norm_rows(r):
            dy = dr[r, :]
            zz = z2[r, :].astype(F32)
            dr2 = norm_pull(zz, s12[m, r, 1:2], g2[...].astype(F32), dy)
            vacc[0] += rowsum8(dy * zz)
            vacc[1] += rowsum8(dy)
            d2 = dr2.astype(BF)
            dr[r, :] = dr2
            db2[m, r, :] = d2
            vacc[2] += rowsum8(d2.astype(F32))

        @pl.when(sec == 0)
        def _():
            def norm_step(i, _):
                r = pl.ds(pl.multiple_of(i * xb, xb), xb)
                handoff(m, i).wait_recv()
                dr[r, :] = dyx[m, r, :].astype(F32)
                norm_rows(r)
                return 0
            lax.fori_loop(0, nx, norm_step, 0)

        @pl.when(sec != 0)
        def _():
            dp3 = jnp.concatenate(split3(jnp.concatenate([dps[pl.ds(pl.multiple_of(m * SL, SL), SL), :], jnp.zeros((16 - SL, D), F32)], axis=0)), axis=0)
            dr[...] = dot_tn(jnp.concatenate([mem, mem, mem], axis=0), dp3)
            for i in range(nb):
                norm_rows(slice(i * tb, (i + 1) * tb))

    def token_pass(m, norms, ins):
        @pl.when(m == 0)
        def _():
            for w in wcp[:3]:
                w.wait()
        norms[1].wait()
        ins[0].wait()
        ins[1].wait()
        for i in range(nb):
            r = slice(i * tb, (i + 1) * tb)
            d2 = db2[m, r, :]
            dh = dr[r, :]
            dfs = [dot_nt(d2, wout[:D, :])]
            for j in range(nj):
                cols = slice(j * D, (j + 1) * D)
                if j + 1 < nj:
                    dfs.append(dot_nt(d2, wout[(j + 1) * D:(j + 2) * D, :]))
                dub = (dfs[j] * gp[m, r, cols].astype(F32)).astype(BF)
                gp[m, r, cols] = dub
                bacc[:, cols] += rowsum8(dub.astype(F32))
                dh = dh + dot_nt(dub, win[:, cols])
            dr[r, :] = dh
            run_when(jnp.logical_and(m == M - 1, sec == 0), AFTER_TOKENS[i])
        for i in range(nb):
            r = slice(i * tb, (i + 1) * tb)
            dh = dr[r, :]
            zz = z1[r, :].astype(F32)
            d1 = norm_pull(zz, s12[m, r, 0:1], g1[...].astype(F32), dh)
            vacc[3] += rowsum8(dh * zz)
            vacc[4] += rowsum8(dh)
            dr[r, :] = d1
            d1 = d1.astype(BF)
            db1[m, r, :] = d1
            vacc[5] += rowsum8(d1.astype(F32))
            dcb = dot_nt(d1, wat[...]).astype(BF)
            dc[r, :] = dcb
            prod = dcb.astype(F32) * c_s[m, r, :].astype(F32)
            hi = prod.astype(BF)
            low = (prod - hi.astype(F32)).astype(BF)
            delta[:, r] = dot_nt(indicator, hi) + dot_nt(indicator, low)
        @pl.when(m < M - 1)
        def _():
            for cp in norm_copies(m + 1):
                cp.start()
        ins[2].wait()

    def attention_pass(m):
        for p in range(HEADS // 2):
            cols = slice(p * 128, (p + 1) * 128)
            kcols = slice(D + p * 128, D + (p + 1) * 128)
            vcols = slice(2 * D + p * 128, 2 * D + (p + 1) * 128)
            q2 = qkv[m, :, cols] * (HEAD_DIM ** -0.5)
            qh = [jnp.where(low_half, q2, qcode[...]), jnp.where(low_half, qcode[...], q2)]
            dc2 = dc[:, cols]
            dqt = jnp.zeros((128, T), F32)
            for i in range(T // kb):
                r = slice(i * kb, (i + 1) * kb)
                k2 = qkv[m, r, kcols]
                v2 = qkv[m, r, vcols]
                kc = kcode[r, :]
                dks, dvs = [], []
                for h in range(2):
                    pick = low_half if h == 0 else jnp.logical_not(low_half)
                    kh = jnp.where(low_half, k2, kc) if h == 0 else jnp.where(low_half, kc, k2)
                    pt = jnp.exp(dot_nt(kh, qh[h]) - lse[m, 2 * p + h:2 * p + h + 1, :])
                    dpt = dot_nt(jnp.where(pick, v2, 0), dc2)
                    da = (pt * (dpt - delta[2 * p + h:2 * p + h + 1, :])).astype(BF)
                    dvs.append(dot(pt.astype(BF), dc2))
                    dks.append(dot(da, q2))
                    dqt = dqt + dot_tn(jnp.where(pick, k2, 0), da)
                qkv[m, r, kcols] = jnp.where(low_half, dks[0], dks[1]).astype(BF)
                qkv[m, r, vcols] = jnp.where(low_half, dvs[0], dvs[1]).astype(BF)
            qkv[m, :, cols] = (jnp.transpose(dqt) * (HEAD_DIM ** -0.5)).astype(BF)
            if AFTER_PAIR[p]:
                run_when(jnp.logical_and(m == M - 1, sec == 0), AFTER_PAIR[p])
        @pl.when(m == 0)
        def _():
            wcp[3].wait()

        def dx_step(i, _):
            r = pl.ds(pl.multiple_of(i * xb, xb), xb)
            dyx[m, r, :] = (dr[r, :] + dot_nt(qkv[m, r, :], wqkv[...])).astype(BF)

            @pl.when(sec != 0)
            def _():
                handoff(m, i).start()
            vacc[6] += rowsum8(qkv[m, r, :D].astype(F32))
            vacc[7] += rowsum8(qkv[m, r, 2 * D:].astype(F32))
            return 0
        lax.fori_loop(0, nx, dx_step, 0)

        @pl.when(sec == 0)
        def _():
            out_copy(m).start()
            dx_copy(m).start()

    lax.fori_loop(0, M + 1, one_pass, 0)

    vec = [remote(va.at[i], vb.at[i], s.at[chunks], r.at[chunks], target) for i, (s, r, target) in enumerate(
        ((send_a, recv_a, sibling), (send_b, recv_b, across), (send_c, recv_c, near), (send_d, recv_d, far)))]

    def vec_step(i):
        vec[i].wait_recv()
        total = va[i] + vb[i]
        if i < 3:
            va[i + 1] = total
            vec[i + 1].start()
        else:
            vec_o[...] = total
    va[0] = jnp.concatenate([jnp.sum(vacc[...], axis=1)]
        + [jnp.sum(bacc[:, j * D:(j + 1) * D], axis=0, keepdims=True) for j in range(nj)] + [jnp.zeros((8 - nj, D), F32)], axis=0)
    vec[0].start()
    for step in BEFORE_Q.split():
        run(step)
    products_q()
    for step in AT_THE_END.split():
        run(step)

    @pl.when(sec == 0)
    def _():
        pool_copy.wait_recv()
        loss_copy.wait_recv()
        pooled_o[...] = pooled_r[:, :half]
        loss_o[...] = loss_r[...]
        for m in range(M):
            dx_copy(m).wait_send()
            out_copy(m).wait()

    @pl.when(sec != 0)
    def _():
        pool_copy.wait_send()
        loss_copy.wait_send()
        pooled_o[...] = pooled_s[:, half:]
        loss_o[...] = loss_s[...]
        for m in range(M):
            for i in range(nx):
                handoff(m, i).wait_send()
            dx_copy(m).wait_recv()
    for v in vec:
        v.wait_send()
    for k in range(chunks):
        copy_b(k).wait_send()
        if k < nj:
            @pl.when(zlow != k % 2)
            def _():
                copy_c(k).wait_send()

            @pl.when(jnp.logical_and(zlow == k % 2, z != k))
            def _():
                copy_d(k).wait_send()
        else:
            copy_c(k).wait_send()
            copy_d(k).wait_send()


def stack_back(seg, pool, pairs, msgs0, stash, weights, tb=256, xb=128, kb=256):
    x, qkv, lse, c, z1, s12, hb, gp, act, z2 = stash
    wqkv, bq, bv, wat, bat, g1, b1, win, bin_, wout, bout, g2, b2 = weights
    M, T, D = c.shape
    N = M * T
    FF = win.shape[1]
    count = lax.axis_size("dp")
    rows = D // count
    chunks = (4 * D + 2 * FF) // D
    SL = 8
    sds = jax.ShapeDtypeStruct
    out_shape = (sds((16, D), F32), sds((M * SL, D // 2), F32), sds((M * SL, 128), F32), sds((rows, 3 * D), F32), sds((rows, D), F32), sds((rows, FF), F32),
        sds((FF // count, D), F32), sds((M, T, D), BF), sds((M, T, D // 2), BF))
    out_specs = (VM,) * 7 + (ANY, ANY)
    V = pltpu.VMEM
    S = pltpu.SemaphoreType.DMA
    nx = T // xb
    nj = FF // D
    piece = (rows, D)
    scratch = [V((M, T, D), BF), V((D, 3 * D), BF), V((D, D), BF), V((D, FF), BF), V((FF, D), BF),
        V((M, T, 3 * D), BF), V((M, T, D), BF), V((T, D), BF), V((M, T, FF), BF), V((T, D), BF),
        V((T, D), F32), V((T, D), BF), V((16, T), F32), V((M, T, D), BF), V((M, T, D), BF), V((8, 8, D), F32), V((8, FF), F32),
        V((count, 16, D // 2 + 128), BF), V((M * SL, D), F32), V((count * SL, 128), F32), V((count * SL, D), F32), V((M * SL, D), F32), V((M * SL, 128), F32), V((M * SL, D), F32), V((M * SL, 128), F32),
        V((T, 128), BF), V((T, 128), BF), V((count, 16, D // 2 + 128), BF), V((2, N, D), BF), V((2, 2, 2, 2, 2) + piece, BF), V((chunks, 2, 2, 2) + piece, BF), V((chunks, 2, 2) + piece, BF),
        V((chunks, 2) + piece, BF), V((chunks,) + piece, BF), V((2, 2) + piece, BF), V((4, 16, D), F32), V((4, 16, D), F32),
        S((M, 5)), S((4,)), S((2 + nj,)), S((M,)), S((M, nx)), S((M, nx)), S((count - 1,)), S((count - 1,)), S((4,)), S((M, 2))]
    scratch += [S((chunks + 1,)) for _ in range(8)]
    in_specs = (VM,) * 6 + (ANY,) * 12 + (VM, VM)
    return pl.pallas_call(functools.partial(back_kernel, tb, xb, kb), out_shape=out_shape, in_specs=in_specs, out_specs=out_specs,
        scratch_shapes=scratch, compiler_params=pltpu.CompilerParams(vmem_limit_bytes=62 * 2**20, collective_id=3, has_side_effects=True),
        name="stack_back")(seg, pool, pairs, msgs0, lse, s12, z2, gp, z1, c, qkv, hb.reshape(N, D), x.reshape(N, D), act,
            wout, win, wat, wqkv, g1, g2)


def finish_kernel(vec, pooled, loss, g_qkv, g_at, g_in, g_out, dx_h, dxr_h,
    pooled_o, loss_o, gx_o, qkv_o, at_o, in_o, out_o, *rest):
    small, buf, sem = rest[:9], rest[9], rest[10]
    sec = lax.axis_index("section")
    me = lax.axis_index("dp")
    half = buf.shape[2]

    @pl.when(sec == 0)
    def _():
        pltpu.make_async_copy(dx_h.at[:, :, pl.ds(0, half)], buf, sem.at[0]).start()

    @pl.when(sec != 0)
    def _():
        pltpu.make_async_copy(dxr_h, buf, sem.at[0]).start()
    for a, b in ((g_qkv, qkv_o), (g_at, at_o), (g_in, in_o), (g_out, out_o)):
        b[...] = a[...]
    SL = 8
    lane = lax.broadcasted_iota(jnp.int32, (SL, 128), 1) == lax.broadcasted_iota(jnp.int32, (SL, 128), 0)
    for m in range(pooled_o.shape[0]):
        pooled_o[m] = pooled[m * SL:m * SL + SEGS, :]
        loss_o[m:m + 1, :] = jnp.sum(jnp.where(lane, loss[m * SL:(m + 1) * SL, :], 0.0), axis=0, keepdims=True)[:, :SEGS]
    D = vec.shape[1]
    width, wide = small[0].shape[1], small[8].shape[1]
    parts = split3(vec[...])

    def columns(start, size):
        pick = lax.broadcasted_iota(jnp.int32, (D, size), 0) == lax.broadcasted_iota(jnp.int32, (D, size), 1) + start
        pick = jnp.where(pick, 1.0, 0.0).astype(BF)
        return (dot(parts[0], pick) + dot(parts[1], pick)) + dot(parts[2], pick)
    v = columns(me * width, 128)
    for i in range(8):
        small[i][...] = v[i:i + 1, :width]
    per = D // wide
    v = columns(lax.rem(me, per) * wide, 256)
    row = lax.broadcasted_iota(jnp.int32, (16, 256), 0) == 8 + lax.div(me, per)
    small[8][...] = jnp.sum(jnp.where(row, v, 0.0), axis=0, keepdims=True)[:, :wide]
    pltpu.make_async_copy(dxr_h, buf, sem.at[0]).wait()
    gx_o[...] = buf[...].astype(F32)


def finish(vec, pooled, loss, g_qkv, g_at, g_in, g_out, dx, dxr):
    M, T, D = dx.shape
    count = lax.axis_size("dp")
    sds = jax.ShapeDtypeStruct
    f = lambda a: sds(a.shape, F32)
    out_shape = (sds((M, SEGS, D // 2), F32), sds((M, SEGS), F32), sds((M, T, D // 2), F32), f(g_qkv), f(g_at), f(g_in), f(g_out)) + tuple(
        sds((1, D // count), F32) for _ in range(8)) + (sds((1, g_in.shape[1] // count), F32),)
    return pl.pallas_call(finish_kernel, out_shape=out_shape, in_specs=(VM,) * 7 + (ANY,) * 2, out_specs=(VM,) * 16,
        scratch_shapes=[pltpu.VMEM((M, T, D // 2), BF), pltpu.SemaphoreType.DMA((1,))],
        compiler_params=pltpu.CompilerParams(vmem_limit_bytes=VMEM_LIMIT), name="finish")(vec, pooled, loss, g_qkv, g_at, g_in, g_out, dx, dxr)


def contrast_head(pool, seg, pairs, all_pairs):
    M, S = pairs.shape
    D = pool.shape[-1]
    counts = jnp.sum((seg[:, :, None] == jnp.arange(SEGS)).astype(F32), axis=1)[:, :, None]
    pooled = pool[:, :SEGS] / counts
    radius = lax.rsqrt(jnp.sum(pooled * pooled, axis=-1, keepdims=True) + UNIT_EPS)
    unit = (pooled * radius).astype(BF)
    every = lax.all_gather(unit, "dp", axis=1, tiled=True)
    total = every.shape[1]
    start = lax.axis_index("dp") * S
    logits = TEMPER * jnp.einsum("mgd,mkd->mgk", every, every, preferred_element_type=F32)
    cols = jnp.arange(total)
    logits = jnp.where(cols[:, None] == cols[None, :], -MASK_FILL, logits)
    peak = jnp.max(logits, axis=-1, keepdims=True)
    exponent = jnp.exp(logits - peak)
    denom = jnp.sum(exponent, axis=-1, keepdims=True)
    target = cols[None, None, :] == all_pairs[:, :, None]
    loss = peak[..., 0] + jnp.log(denom[..., 0]) - jnp.sum(jnp.where(target, logits, 0.0), axis=-1)
    dl = (exponent / denom - target.astype(F32)).astype(BF)
    rows = lax.dynamic_slice_in_dim(dl, start, S, 1)
    columns = lax.dynamic_slice_in_dim(dl, start, S, 2)
    dn = TEMPER * (jnp.einsum("mgk,mkd->mgd", rows, every, preferred_element_type=F32)
        + jnp.einsum("mkg,mkd->mgd", columns, every, preferred_element_type=F32))
    dp = radius * dn - radius * radius * radius * jnp.sum(pooled * dn, axis=-1, keepdims=True) * pooled
    loss = lax.dynamic_slice_in_dim(loss, start, S, 1)
    return pooled, loss, jnp.pad(dp / counts, ((0, 0), (0, 16 - SEGS), (0, 0)))


def scattered(grads):
    count = lax.axis_size("dp")
    packed = jnp.concatenate([g.reshape(count, -1) for g in grads], axis=1)
    part = lax.psum_scatter(packed, "dp", scatter_dimension=0, tiled=True)[0].astype(F32)
    outs, at = [], 0
    for g in grads:
        size = g.size // count
        outs.append(part[at:at + size].reshape((1, g.shape[0] // count) + g.shape[1:]))
        at += size
    return outs


def swapped(value):
    return lax.ppermute(value, "section", [(0, 1), (1, 0)])


def local(hidden_in, seg_ids, pair_ids, w_qkv, b_query, b_value, w_attn_out, b_attn_out, ln1_gain, ln1_bias, w_in, b_in, w_out, b_out, ln2_gain, ln2_bias):
    M, _, T, D = hidden_in.shape
    sec = lax.axis_index("section")
    first = sec == 0
    weights = (w_qkv[0], b_query, b_value, w_attn_out[0], b_attn_out, ln1_gain, ln1_bias, w_in[0], b_in, w_out[0], b_out, ln2_gain, ln2_bias)
    half = D // 2
    count = lax.axis_size("dp")
    pool, x, qkv, lse, c, z1, s12, hb, gp, act, z2, msgs = stack_fwd(hidden_in[:, 0], seg_ids, pair_ids, weights, count if count == 16 else 0)
    if count == 16:
        parts = stack_back(seg_ids, pool, pair_ids, msgs, (x, qkv, lse, c, z1, s12, hb, gp, act, z2), weights)
        pooled, loss, grad_input, g_qkv, g_at, g_in, g_out, gg2, gb2, gbo, gg1, gb1, gba, gbq, gbv, gbi = finish(*parts)
        pooled_out, loss_out = pooled, loss
        g_qkv, g_at, g_in, g_out = (g[None] for g in (g_qkv, g_at, g_in, g_out))
    else:
        seg = seg_ids[:, 0]
        all_pairs = lax.all_gather(pair_ids, "dp", axis=1, tiled=True)
        pooled, loss, dp = contrast_head(pool, seg, pair_ids, all_pairs)
        vec, dx, dxb, db2, du, db1, dqkv = stack_bwd(seg, dp, (qkv, lse, c, z1, s12, gp, z2), weights)
        act = jnp.moveaxis(act, 0, 1).reshape(M, T, -1)
        big = [jnp.einsum("mta,mtb->ab", a, b, preferred_element_type=F32).astype(BF) for a, b in ((x, dqkv), (c, db1), (hb, du), (act, db2))]
        g_qkv, g_at, g_in, g_out = scattered(big)
        small = scattered([vec[i] for i in range(8)] + [vec[8:8 + w_in.shape[2] // D].reshape(-1)])
        gg2, gb2, gbo, gg1, gb1, gba, gbq, gbv, gbi = small
        kept = lax.dynamic_slice_in_dim(dx, sec * half, half, 2)
        sent = lax.dynamic_slice_in_dim(dxb, (1 - sec) * half, half, 2)
        grad_input = jnp.where(first, kept, swapped(sent).astype(F32))
        pooled_kept = lax.dynamic_slice_in_dim(pooled, sec * half, half, 2)
        pooled_sent = lax.dynamic_slice_in_dim(pooled, (1 - sec) * half, half, 2).astype(BF)
        pooled_out = jnp.where(first, swapped(pooled_sent).astype(F32), pooled_kept)
        loss_out = jnp.where(first, swapped(loss.astype(BF)).astype(F32), loss)
    return (pooled_out, loss_out, grad_input[:, None], g_qkv, gbq, gbv, g_at, gba, gg1, gb1, g_in, gbi, g_out, gbo, gg2, gb2)


def solution(mesh):
    in_specs = (
        P(None, "dp", None, None),
        P(None, "dp", None),
        P(None, "dp"),
        P("section", None, None),
        P("section", None),
        P("section", None),
        P("section", None, None),
        P("section", None),
        P("section", None),
        P("section", None),
        P("section", None, None),
        P("section", None),
        P("section", None, None),
        P("section", None),
        P("section", None),
        P("section", None),
    )
    out_specs = (
        P(None, "dp", "section"),
        P(None, "dp"),
        P(None, "dp", None, "section"),
        P("section", "dp", None),
        P("section", "dp"),
        P("section", "dp"),
        P("section", "dp", None),
        P("section", "dp"),
        P("section", "dp"),
        P("section", "dp"),
        P("section", "dp", None),
        P("section", "dp"),
        P("section", "dp", None),
        P("section", "dp"),
        P("section", "dp"),
        P("section", "dp"),
    )
    return jax.shard_map(local, mesh=mesh, in_specs=in_specs, out_specs=out_specs, check_vma=False)
```

profile of v0, /device:TPU:0, one launch (start us, length us, event | category | flops | bytes accessed | tf_op | source)
XLA Modules:
  0.0 246.6 jit_solution(10164927915617077857)
XLA Ops:
  0.6 51.1 %stack_fwd.1 = (f32[2,16,768]{2,1,0:T(8,128)}, bf16[2,512,768]{2,1,0:T(8,128)(2,1)}, bf16[2,512,2304]{2,1,0:T(8,128)(2,1)}, f32[2,16,512]{2,1,0:T(8,128)}, bf16[...) custom-call(bf16[2,512,768]{2,1,0:T(8,128)(2,1)} %bitcast.24, ...), custom_call_target="tpu_custom_call" | custom-call | tf_op jit(solution)/shard_map/stack_fwd/pallas_call | solution.py:288
  51.7 190.1 %stack_back.1 = (f32[16,768]{1,0:T(8,128)}, f32[16,384]{1,0:T(8,128)}, f32[16,128]{1,0:T(8,128)}, f32[48,2304]{1,0:T(8,128)}, f32[48,768]{1,0:T(8,128)}, /*index...) custom-call(s32[2,1,512]{2,1,0:T(1,128)} %seg.3, ...), custom_call_target="tpu_custom_call" | custom-call | tf_op jit(solution)/shard_map/stack_back/pallas_call | solution.py:1091
  241.9 4.5 %finish.1 = (f32[2,4,384]{2,1,0:T(4,128)}, f32[2,4]{1,0:T(2,128)}, f32[2,512,384]{2,1,0:T(8,128)}, f32[48,2304]{1,0:T(8,128)}, f32[48,768]{1,0:T(8,128)}, /*inde...) custom-call(f32[16,768]{1,0:T(8,128)} %get-tuple-element.65.vec, ...), custom_call_target="tpu_custom_call" | custom-call | tf_op jit(solution)/shard_map/finish/pallas_call | solution.py:1144
where the time goes:
time: 247 us
  Pallas kernels  246 us (100%)
    pallas_call x1, Pallas kernels, stack_back(): pl.pallas_call(functools.partial(back_kernel, tb, xb, kb), out_shape=out_...  190 us
    pallas_call x1, Pallas kernels, stack_fwd(): pl.pallas_call(functools.partial(fwd_kernel, tb, fc, peers), out_shape=ou...  51.1 us

commit v1 on v0

--- a/solution.py
+++ b/solution.py
@@ -84,7 +84,7 @@
     return jnp.concatenate([jnp.concatenate([unit[:, :half], tag], axis=1), jnp.concatenate([unit[:, half:], tag], axis=1)], axis=0).astype(BF)
 
 
-def fwd_kernel(tb, fc, peers,
+def fwd_kernel(tb, peers,
     x_h, seg, pairs, wqkv_h, bq, bv, wat_h, bat, g1, b1, win_h, bin_, wout_h, bout, g2, b2,
     pool_o, x_o, qkv_h, lse_o, c_h, z1_h, s12_o, hb_h, gp_h, act_h, z2_h, msgs_o,
     x_s, wqkv, wat, win, wout, qkv, c_s, hb_s, z1_s, gp_s, act_s, z2_s, y_s, yf, msgs, kcode, qcode,
@@ -107,13 +107,6 @@
     pl.semaphore_signal(barrier, inc=1, device_id=other, device_id_type=MESH)
     for d in range(1, peers):
         pl.semaphore_signal(barrier, inc=1, device_id={"dp": lax.rem(me + d, peers)}, device_id_type=MESH)
-    for w in ws[1:]:
-        w.start()
-
-    @pl.when(sec == 0)
-    def _():
-        for m in range(1, M):
-            pltpu.make_async_copy(x_h.at[m], x_s.at[m], insem.at[m]).start()
 
     lane = lax.broadcasted_iota(jnp.int32, (1, 128), 1)
     low_half = lane < HEAD_DIM
@@ -123,10 +116,14 @@
 
     def out_copies(m, i):
         r = block(i * tb)
-        span = block(m * T + i * tb)
-        pairs = [(a.at[m, r], b.at[m, r]) for a, b in ((c_s, c_h), (hb_s, hb_h), (z1_s, z1_h), (z2_s, z2_h), (gp_s, gp_h))]
-        pairs += [(act_s.at[m, r, j * D:(j + 1) * D], act_h.at[j, span]) for j in range(FF // D)]
-        return [pltpu.make_async_copy(a, b, outsem.at[m, i, j]) for j, (a, b) in enumerate(pairs)]
+        return [pltpu.make_async_copy(a.at[m, r], b.at[m, r], outsem.at[m, i, j]) for j, (a, b) in enumerate(
+            ((c_s, c_h), (hb_s, hb_h), (z1_s, z1_h), (z2_s, z2_h)))]
+
+    def wide_copies(m, i, j):
+        r = block(i * tb)
+        cols = slice(j * D, (j + 1) * D)
+        return [pltpu.make_async_copy(gp_s.at[m, r, cols], gp_h.at[m, r, cols], outsem.at[m, i, 4 + 2 * j]),
+            pltpu.make_async_copy(act_s.at[m, r, cols], act_h.at[j, block(m * T + i * tb)], outsem.at[m, i, 5 + 2 * j])]
 
     def whole_copies(m):
         return [pltpu.make_async_copy(a.at[m], b.at[m], outsem.at[m, nb, j]) for j, (a, b) in enumerate(((x_s, x_o), (qkv, qkv_h)))]
@@ -151,18 +148,29 @@
         @pl.when(m == 0)
         def _():
             ws[0].wait()
-
-        @pl.when(sec != 0)
-        def _():
-            for i in range(nb):
+            for w in ws[1:]:
+                w.start()
+
+            @pl.when(sec == 0)
+            def _():
+                for n in range(1, M):
+                    pltpu.make_async_copy(x_h.at[n], x_s.at[n], insem.at[n]).start()
+
+        def qkv_step(i, _):
+            r = block(i * tb)
+
+            @pl.when(sec != 0)
+            def _():
                 handoff(m, i).wait_recv()
-        xi = x_s[m]
-        for j, b in ((0, bq), (1, None), (2, bv)):
-            cols = slice(j * D, (j + 1) * D)
-            v = dot(xi, wqkv[:, cols])
-            if b is not None:
-                v = v + b[...].astype(F32)
-            qkv[m, :, cols] = v.astype(BF)
+            xi = x_s[m, r, :]
+            for j, b in ((0, bq), (1, None), (2, bv)):
+                cols = slice(j * D, (j + 1) * D)
+                v = dot(xi, wqkv[:, cols])
+                if b is not None:
+                    v = v + b[...].astype(F32)
+                qkv[m, r, cols] = v.astype(BF)
+            return 0
+        lax.fori_loop(0, nb, qkv_step, 0)
         for cp in whole_copies(m):
             cp.start()
         ones = jnp.ones((T, 128), BF)
@@ -203,18 +211,23 @@
             hb_s[m, r, :] = hi
             z1_s[m, r, :] = z.astype(BF)
             s12_o[m, r, 0:1] = scale
+            outs = out_copies(m, i)
+            for cp in outs[:3]:
+                cp.start()
             acc = acc + bout[...].astype(F32)
-            nj = FF // fc
-            us = [dot(hi, win[:, :fc])]
+            nj = FF // D
+            us = [dot(hi, win[:, :D])]
             for j in range(nj):
-                cols = slice(j * fc, (j + 1) * fc)
+                cols = slice(j * D, (j + 1) * D)
                 if j + 1 < nj:
-                    us.append(dot(hi, win[:, (j + 1) * fc:(j + 2) * fc]))
+                    us.append(dot(hi, win[:, (j + 1) * D:(j + 2) * D]))
                 f, gp = gelu_pair(us[j] + bin_[:, cols].astype(F32))
                 f = f.astype(BF)
                 act_s[m, r, cols] = f
                 gp_s[m, r, cols] = gp.astype(BF)
                 acc = acc + dot(f, wout[cols, :])
+                for cp in wide_copies(m, i, j):
+                    cp.start()
             z, scale = normed_rows(acc)
             y = z * g2[...].astype(F32) + b2[...].astype(F32)
             y_s[m, r, :] = y.astype(BF)
@@ -225,8 +238,7 @@
             z2_s[m, r, :] = z.astype(BF)
             s12_o[m, r, 1:2] = scale
             yf[r, :] = y
-            for cp in out_copies(m, i):
-                cp.start()
+            outs[3].start()
             return 0
         lax.fori_loop(0, nb, block_step, 0)
 
@@ -260,7 +272,7 @@
         for cp in whole_copies(m):
             cp.wait()
         for i in range(nb):
-            for cp in out_copies(m, i):
+            for cp in out_copies(m, i) + sum((wide_copies(m, i, j) for j in range(FF // D)), []):
                 cp.wait()
 
     @pl.when(sec == 0)
@@ -270,7 +282,7 @@
                 handoff(m, i).wait_send()
 
 
-def stack_fwd(x, seg, pairs, weights, peers, tb=256, fc=768):
+def stack_fwd(x, seg, pairs, weights, peers, tb=256):
     M, T, D = x.shape
     FF = weights[7].shape[1]
     sds = jax.ShapeDtypeStruct
@@ -282,10 +294,10 @@
     nb = T // tb
     scratch = [V((M, T, D), BF), V((D, 3 * D), BF), V((D, D), BF), V((D, FF), BF), V((FF, D), BF), V((M, T, 3 * D), BF),
         V((M, T, D), BF), V((M, T, D), BF), V((M, T, D), BF), V((M, T, FF), BF), V((M, T, FF), BF), V((M, T, D), BF), V((M, T, D), BF),
-        V((T, D), F32), V((max(peers, 1), 16, D // 2 + 128), BF), V((T, 128), BF), V((T, 128), BF), S((M,)), S((4,)), S((M, nb + 1, 5 + FF // D)), S((M, nb)), S((M, nb)),
+        V((T, D), F32), V((max(peers, 1), 16, D // 2 + 128), BF), V((T, 128), BF), V((T, 128), BF), S((M,)), S((4,)), S((M, nb + 1, 4 + 2 * (FF // D))), S((M, nb)), S((M, nb)),
         S((max(peers, 2) - 1,)), S((max(peers, 2) - 1,))]
     in_specs = (ANY, VM, VM, ANY, VM, VM, ANY, VM, VM, VM, ANY, VM, ANY, VM, VM, VM)
-    return pl.pallas_call(functools.partial(fwd_kernel, tb, fc, peers), out_shape=out_shape, in_specs=in_specs, out_specs=out_specs,
+    return pl.pallas_call(functools.partial(fwd_kernel, tb, peers), out_shape=out_shape, in_specs=in_specs, out_specs=out_specs,
         scratch_shapes=scratch, compiler_params=pltpu.CompilerParams(vmem_limit_bytes=VMEM_LIMIT, collective_id=0, has_side_effects=True),
         name="stack_fwd")(x, seg, pairs, *weights)
 
@@ -500,13 +512,13 @@
         name="stack_bwd")(seg, dp, lse, s12, qkv, c, z1, gp, z2, wqkv, wat, g1, win, wout, g2)
 
 
-AFTER_TOKENS = (" ".join(("a2 a3 b0",)), " ".join(("b1",)))
-AFTER_W = ("", " ".join(("a4 c0",)), " ".join(("a5 b2",)), " ".join(("a6 c1",)))
+AFTER_TOKENS = ("", " ".join(("a2 a3 b0",)))
+AFTER_W = ("", " ".join(("a4 b1",)), " ".join(("a5",)), " ".join(("a6 b2 c0",)))
 AFTER_A = " ".join(("b3",))
-AFTER_PAIR = (" ".join(("a7",)), " ".join(("a8 c2",)), " ".join(("b4",)), "", " ".join(("c3",)), "")
-BEFORE_Q = " ".join(("b5 b8",))
-AFTER_Q = ("", " ".join(("v0 a9 c4 b6",)), "")
-AT_THE_END = " ".join(("v1 a10 c5 d3", "b7 a11 c8 d4", "c6 b9 d5 c7", "v2 b10 d6 c9", "v3 d7 b11 c10", "d8 d9 c11 d10", "d11",))
+AFTER_PAIR = (" ".join(("a7 c1",)), "", "", " ".join(("b4",)), " ".join(("a8",)), "")
+BEFORE_Q = " ".join(("c2 b5",))
+AFTER_Q = ("", " ".join(("v0 a9 c3 c4", "b6",)), "")
+AT_THE_END = " ".join(("v1 a10 b8 b7", "c5 a11 d4 b9", "d3 c6 c8 b10", "c7 v2 d5 b11", "c9 v3 b12 d8", "d6 c10 d7 c11", "d9 c12 d10 d11", "d12",))
 
 
 def back_kernel(tb, xb, kb,
@@ -543,6 +555,7 @@
     rows = got_a.shape[4]
     SL = 8
     zchunk = 2 * nj
+    cut = rows // 48 * 32
 
     wcp = [pltpu.make_async_copy(a, b, wsem.at[i]) for i, (a, b) in enumerate(
         ((wout_h, wout), (win_h, win), (wat_h, wat), (wqkv_h, wqkv)))]
@@ -565,13 +578,8 @@
     pl.semaphore_signal(barrier, inc=1, device_id=other, device_id_type=MESH)
     for d in range(1, peers):
         pl.semaphore_signal(barrier, inc=1, device_id={"dp": lax.rem(me + d, peers)}, device_id_type=MESH)
-    for a in [ins[0], wcp[1], norms[1], wcp[2], ins[1], ins[2], wcp[3]]:
+    for a in [ins[0], wcp[1], norms[1], wcp[2], ins[1]]:
         a.start()
-    for m in range(1, M):
-        for a in in_copies(m):
-            a.start()
-    act_copy(0).start()
-    act_copy(1).start()
     vacc[...] = jnp.zeros_like(vacc)
     bacc[...] = jnp.zeros_like(bacc)
 
@@ -579,8 +587,6 @@
         return remote(msgs.at[me], msgs.at[me], msg_send.at[d - 1], msg_recv.at[d - 1], {"dp": lax.rem(me + d, peers)})
     pool_copy = remote(pooled_s, pooled_r, pool_sem.at[0], pool_sem.at[1], other)
     loss_copy = remote(loss_s, loss_r, pool_sem.at[2], pool_sem.at[3], other)
-    pl.semaphore_wait(barrier, peers)
-
     def head(m):
         eight = pl.ds(pl.multiple_of(m * SL, SL), SL)
         pooled, radius, counts = documents(members(seg[m]), pool[m])
@@ -608,17 +614,6 @@
         loss_s[eight, :] = loss_w[own, :]
         dps[eight, :] = (radius * dn - radius * radius * radius * jnp.sum(pooled * dn, axis=-1, keepdims=True) * pooled) / counts
 
-    @pl.when(sec != 0)
-    def _():
-        for m in range(M):
-            pooled, radius, _ = documents(members(seg[m]), pool[m])
-            pooled_s[m * SL:(m + 1) * SL, :] = pooled
-            if m == 1:
-                msgs[me] = message(pooled * radius, pairs[m:m + 1, :])
-        for d in range(1, peers):
-            msg_copy(d).start()
-        pool_copy.start()
-
     lane = lax.broadcasted_iota(jnp.int32, (1, 128), 1)
     low_half = lane < HEAD_DIM
     indicator = jnp.where(lax.broadcasted_iota(jnp.int32, (16, D), 1) // HEAD_DIM == lax.broadcasted_iota(jnp.int32, (16, D), 0), 1.0, 0.0).astype(BF)
@@ -637,6 +632,12 @@
         g = dy * gain
         return scale * (g - jnp.mean(g, axis=-1, keepdims=True) - zz * jnp.mean(g * zz, axis=-1, keepdims=True))
 
+    def base(k):
+        return min(k, chunks - 1)
+
+    def span(k):
+        return pl.ds(0, cut) if k == chunks - 1 else pl.ds(cut, rows - cut) if k == chunks else pl.ds(0, rows)
+
     def slot(k):
         return k % 2 if isinstance(k, int) else lax.rem(k, 2)
 
@@ -645,6 +646,8 @@
 
     def copy_b(k):
         if not isinstance(k, int) or k != zchunk:
+            if isinstance(k, int) and k >= nj:
+                return remote(got_a.at[base(k), :, :, 1 - y, span(k)], got_b.at[base(k), :, :, span(k)], send_b.at[k], recv_b.at[k], across)
             return remote(got_a.at[k, :, :, 1 - y], got_b.at[k], send_b.at[k], recv_b.at[k], across)
         return remote(got_a.at[k, zhigh, zlow, 1 - y], got_d.at[k], send_b.at[k], recv_b.at[k], across)
 
@@ -653,14 +656,14 @@
             return remote(got_b.at[k], got_c.at[pl.ds(2 * (k // 2), 2)], send_c.at[k], recv_c.at[k], near)
         if k == zchunk:
             return remote(got_a.at[k, :, 1 - zlow], got_b.at[k], send_c.at[k], recv_c.at[k], near)
-        return remote(got_b.at[k, :, 1 - zlow], got_c.at[k], send_c.at[k], recv_c.at[k], near)
+        return remote(got_b.at[base(k), :, 1 - zlow, span(k)], got_c.at[base(k), :, span(k)], send_c.at[k], recv_c.at[k], near)
 
     def copy_d(k):
         if not isinstance(k, int) or k < nj:
             return remote(got_b.at[k], got_t, send_d.at[k], recv_d.at[k], far)
         if k == zchunk:
             return remote(got_a.at[k, 1 - zhigh, zlow], got_c.at[k], send_d.at[k], recv_d.at[k], far)
-        return remote(got_b.at[k, 1 - zhigh, zlow], got_d.at[k], send_d.at[k], recv_d.at[k], far)
+        return remote(got_b.at[base(k), 1 - zhigh, zlow, span(k)], got_d.at[base(k), span(k)], send_d.at[k], recv_d.at[k], far)
 
     def e1(k):
         copy_a(k).wait_recv()
@@ -671,6 +674,8 @@
             copy_c(k).start()
         else:
             copy_b(k).start()
+            if isinstance(k, int) and k == chunks - 1:
+                copy_b(chunks).start()
         copy_a(k).wait_send()
 
     def e2(k):
@@ -682,7 +687,10 @@
             return
         copy_b(k).wait_recv()
         for h in range(2):
-            got_b[k, h] = got_b[k, h] + got_a[k, h, :, y]
+            if k < nj:
+                got_b[k, h] = got_b[k, h] + got_a[k, h, :, y]
+            else:
+                got_b[base(k), h, :, span(k)] = got_b[base(k), h, :, span(k)] + got_a[base(k), h, :, y, span(k)]
         if k < nj:
             @pl.when(zlow != k % 2)
             def _():
@@ -708,7 +716,7 @@
         else:
             copy_c(k).wait_recv()
             for h in range(2):
-                got_b[k, h, zlow] = got_b[k, h, zlow] + got_c[k, h]
+                got_b[base(k), h, zlow, span(k)] = got_b[base(k), h, zlow, span(k)] + got_c[base(k), h, span(k)]
             copy_d(k).start()
 
     def e4(k):
@@ -716,7 +724,7 @@
             copy_b(k).wait_recv()
             return got_a[k, zhigh, zlow, y].astype(F32) + got_d[k].astype(F32)
         copy_d(k).wait_recv()
-        return got_b[k, zhigh, zlow].astype(F32) + got_d[k].astype(F32)
+        return got_b[base(k), zhigh, zlow, span(k)].astype(F32) + got_d[base(k), span(k)].astype(F32)
 
     def tile_out(k, lhs, right):
         def side(i, _):
@@ -798,7 +806,7 @@
         elif k == 2 * nj:
             g_at[...] = v
         else:
-            g_qkv[:, (k - 2 * nj - 1) * D:(k - 2 * nj) * D] = v
+            g_qkv[span(k), (base(k) - 2 * nj - 1) * D:(base(k) - 2 * nj) * D] = v
 
     def store_w_out():
         copy_d(z).wait_recv()
@@ -873,10 +881,6 @@
                 gathered[...] = msgs[...]
             head(m)
 
-            @pl.when(m == M - 1)
-            def _():
-                loss_copy.start()
-
         def norm_rows(r):
             dy = dr[r, :]
             zz = z2[r, :].astype(F32)
@@ -905,11 +909,37 @@
             for i in range(nb):
                 norm_rows(slice(i * tb, (i + 1) * tb))
 
+        @pl.when(m == 0)
+        def _():
+            pl.semaphore_wait(barrier, peers)
+
+            @pl.when(sec != 0)
+            def _():
+                for m in range(M):
+                    pooled, radius, _ = documents(members(seg[m]), pool[m])
+                    pooled_s[m * SL:(m + 1) * SL, :] = pooled
+                    if m == 1:
+                        msgs[me] = message(pooled * radius, pairs[m:m + 1, :])
+                for d in range(1, peers):
+                    msg_copy(d).start()
+                pool_copy.start()
+
     def token_pass(m, norms, ins):
+        @pl.when(jnp.logical_and(m == M - 1, sec != 0))
+        def _():
+            loss_copy.start()
+
         @pl.when(m == 0)
         def _():
             for w in wcp[:3]:
                 w.wait()
+            in_copies(0)[2].start()
+            wcp[3].start()
+            for n in range(1, M):
+                for a in in_copies(n):
+                    a.start()
+            act_copy(0).start()
+            act_copy(1).start()
         norms[1].wait()
         ins[0].wait()
         ins[1].wait()
@@ -1003,7 +1033,7 @@
 
     lax.fori_loop(0, M + 1, one_pass, 0)
 
-    vec = [remote(va.at[i], vb.at[i], s.at[chunks], r.at[chunks], target) for i, (s, r, target) in enumerate(
+    vec = [remote(va.at[i], vb.at[i], s.at[chunks + 1], r.at[chunks + 1], target) for i, (s, r, target) in enumerate(
         ((send_a, recv_a, sibling), (send_b, recv_b, across), (send_c, recv_c, near), (send_d, recv_d, far)))]
 
     def vec_step(i):
@@ -1045,7 +1075,7 @@
             dx_copy(m).wait_recv()
     for v in vec:
         v.wait_send()
-    for k in range(chunks):
+    for k in range(chunks + 1):
         copy_b(k).wait_send()
         if k < nj:
             @pl.when(zlow != k % 2)
@@ -1086,7 +1116,7 @@
         V((T, 128), BF), V((T, 128), BF), V((count, 16, D // 2 + 128), BF), V((2, N, D), BF), V((2, 2, 2, 2, 2) + piece, BF), V((chunks, 2, 2, 2) + piece, BF), V((chunks, 2, 2) + piece, BF),
         V((chunks, 2) + piece, BF), V((chunks,) + piece, BF), V((2, 2) + piece, BF), V((4, 16, D), F32), V((4, 16, D), F32),
         S((M, 5)), S((4,)), S((2 + nj,)), S((M,)), S((M, nx)), S((M, nx)), S((count - 1,)), S((count - 1,)), S((4,)), S((M, 2))]
-    scratch += [S((chunks + 1,)) for _ in range(8)]
+    scratch += [S((chunks + 2,)) for _ in range(8)]
     in_specs = (VM,) * 6 + (ANY,) * 12 + (VM, VM)
     return pl.pallas_call(functools.partial(back_kernel, tb, xb, kb), out_shape=out_shape, in_specs=in_specs, out_specs=out_specs,
         scratch_shapes=scratch, compiler_params=pltpu.CompilerParams(vmem_limit_bytes=62 * 2**20, collective_id=3, has_side_effects=True),
@@ -1096,7 +1126,10 @@
 
 def finish_kernel(vec, pooled, loss, g_qkv, g_at, g_in, g_out, dx_h, dxr_h,
     pooled_o, loss_o, gx_o, qkv_o, at_o, in_o, out_o, *rest):
-    small, buf, sem = rest[:9], rest[9], rest[10]
+    small, buf, wide_buf, bufs, sem = rest[:9], rest[9], rest[10], rest[11:15], rest[15]
+    came = [pltpu.make_async_copy(a, b, sem.at[1 + i]) for i, (a, b) in enumerate(zip((g_qkv, g_at, g_in, g_out), bufs))]
+    goes = [pltpu.make_async_copy(b, a, sem.at[5 + i]) for i, (a, b) in enumerate(zip((qkv_o, at_o, in_o, out_o), bufs))]
+    goes += [pltpu.make_async_copy(wide_buf, gx_o, sem.at[9])]
     sec = lax.axis_index("section")
     me = lax.axis_index("dp")
     half = buf.shape[2]
@@ -1108,8 +1141,14 @@
     @pl.when(sec != 0)
     def _():
         pltpu.make_async_copy(dxr_h, buf, sem.at[0]).start()
-    for a, b in ((g_qkv, qkv_o), (g_at, at_o), (g_in, in_o), (g_out, out_o)):
-        b[...] = a[...]
+    for cp in came:
+        cp.start()
+    pltpu.make_async_copy(dxr_h, buf, sem.at[0]).wait()
+    wide_buf[...] = buf[...].astype(F32)
+    goes[4].start()
+    for a, b in zip(came, goes):
+        a.wait()
+        b.start()
     SL = 8
     lane = lax.broadcasted_iota(jnp.int32, (SL, 128), 1) == lax.broadcasted_iota(jnp.int32, (SL, 128), 0)
     for m in range(pooled_o.shape[0]):
@@ -1130,8 +1169,8 @@
     v = columns(lax.rem(me, per) * wide, 256)
     row = lax.broadcasted_iota(jnp.int32, (16, 256), 0) == 8 + lax.div(me, per)
     small[8][...] = jnp.sum(jnp.where(row, v, 0.0), axis=0, keepdims=True)[:, :wide]
-    pltpu.make_async_copy(dxr_h, buf, sem.at[0]).wait()
-    gx_o[...] = buf[...].astype(F32)
+    for cp in goes:
+        cp.wait()
 
 
 def finish(vec, pooled, loss, g_qkv, g_at, g_in, g_out, dx, dxr):
@@ -1141,8 +1180,9 @@
     f = lambda a: sds(a.shape, F32)
     out_shape = (sds((M, SEGS, D // 2), F32), sds((M, SEGS), F32), sds((M, T, D // 2), F32), f(g_qkv), f(g_at), f(g_in), f(g_out)) + tuple(
         sds((1, D // count), F32) for _ in range(8)) + (sds((1, g_in.shape[1] // count), F32),)
-    return pl.pallas_call(finish_kernel, out_shape=out_shape, in_specs=(VM,) * 7 + (ANY,) * 2, out_specs=(VM,) * 16,
-        scratch_shapes=[pltpu.VMEM((M, T, D // 2), BF), pltpu.SemaphoreType.DMA((1,))],
+    return pl.pallas_call(finish_kernel, out_shape=out_shape, in_specs=(VM,) * 3 + (ANY,) * 6, out_specs=(VM,) * 2 + (ANY,) * 5 + (VM,) * 9,
+        scratch_shapes=[pltpu.VMEM((M, T, D // 2), BF), pltpu.VMEM((M, T, D // 2), F32)] + [pltpu.VMEM(g.shape, F32) for g in (g_qkv, g_at, g_in, g_out)]
+        + [pltpu.SemaphoreType.DMA((10,))],
         compiler_params=pltpu.CompilerParams(vmem_limit_bytes=VMEM_LIMIT), name="finish")(vec, pooled, loss, g_qkv, g_at, g_in, g_out, dx, dxr)
 
 

time: 247 us -> 241 us (0.976)
  Pallas kernels: 246 us -> 238 us
    pallas_call x1, Pallas kernels: 190 us -> 181 us  [stack_back(): pl.pallas_call(functools.partial(back_kernel, tb, xb, kb), out_shape=out_...]
where the time goes in v1:
time: 241 us; the launch traced here: 239 us
  Pallas kernels  238 us (99%)
    pallas_call x1, Pallas kernels, stack_back(): pl.pallas_call(functools.partial(back_kernel, tb, xb, kb), out_shape=out_...  181 us
    pallas_call x1, Pallas kernels, stack_fwd(): pl.pallas_call(functools.partial(fwd_kernel, tb, peers), out_shape=out_sh...  52 us

profile of v1, /device:TPU:0, one launch (start us, length us, event | category | flops | bytes accessed | tf_op | source)
XLA Modules:
  0.0 238.8 jit_solution(7933000247775993290)
XLA Ops:
  0.6 52.0 %stack_fwd.1 = (f32[2,16,768]{2,1,0:T(8,128)}, bf16[2,512,768]{2,1,0:T(8,128)(2,1)}, bf16[2,512,2304]{2,1,0:T(8,128)(2,1)}, f32[2,16,512]{2,1,0:T(8,128)}, bf16[...) custom-call(bf16[2,512,768]{2,1,0:T(8,128)(2,1)} %bitcast.24, ...), custom_call_target="tpu_custom_call" | custom-call | tf_op jit(solution)/shard_map/stack_fwd/pallas_call | solution.py:300
  52.7 181.4 %stack_back.1 = (f32[16,768]{1,0:T(8,128)}, f32[16,384]{1,0:T(8,128)}, f32[16,128]{1,0:T(8,128)}, f32[48,2304]{1,0:T(8,128)}, f32[48,768]{1,0:T(8,128)}, /*index...) custom-call(s32[2,1,512]{2,1,0:T(1,128)} %seg.3, ...), custom_call_target="tpu_custom_call" | custom-call | tf_op jit(solution)/shard_map/stack_back/pallas_call | solution.py:1121
  234.1 4.5 %finish.1 = (f32[2,4,384]{2,1,0:T(4,128)}, f32[2,4]{1,0:T(2,128)}, f32[2,512,384]{2,1,0:T(8,128)}, f32[48,2304]{1,0:T(8,128)}, f32[48,768]{1,0:T(8,128)}, /*inde...) custom-call(f32[16,768]{1,0:T(8,128)} %get-tuple-element.65.vec, ...), custom_call_target="tpu_custom_call" | custom-call | tf_op jit(solution)/shard_map/finish/pallas_call | solution.py:1183

commit v2 on v1

--- a/solution.py
+++ b/solution.py
@@ -1090,7 +1090,7 @@
             copy_d(k).wait_send()
 
 
-def stack_back(seg, pool, pairs, msgs0, stash, weights, tb=256, xb=128, kb=256):
+def stack_back(seg, pool, pairs, msgs0, stash, weights, tb=256, xb=256, kb=256):
     x, qkv, lse, c, z1, s12, hb, gp, act, z2 = stash
     wqkv, bq, bv, wat, bat, g1, b1, win, bin_, wout, bout, g2, b2 = weights
     M, T, D = c.shape

time: 241 us -> 238 us (0.988)
  no operation moved by 1% of the time
where the time goes in v2:
time: 238 us
  Pallas kernels  237 us (100%)
    pallas_call x1, Pallas kernels, stack_back(): pl.pallas_call(functools.partial(back_kernel, tb, xb, kb), out_shape=out_...  180 us
    pallas_call x1, Pallas kernels, stack_fwd(): pl.pallas_call(functools.partial(fwd_kernel, tb, peers), out_shape=out_sh...  52 us

profile of v2, /device:TPU:0, one launch (start us, length us, event | category | flops | bytes accessed | tf_op | source)
XLA Modules:
  0.0 237.8 jit_solution(13300637275428281799)
XLA Ops:
  0.6 52.0 %stack_fwd.1 = (f32[2,16,768]{2,1,0:T(8,128)}, bf16[2,512,768]{2,1,0:T(8,128)(2,1)}, bf16[2,512,2304]{2,1,0:T(8,128)(2,1)}, f32[2,16,512]{2,1,0:T(8,128)}, bf16[...) custom-call(bf16[2,512,768]{2,1,0:T(8,128)(2,1)} %bitcast.24, ...), custom_call_target="tpu_custom_call" | custom-call | tf_op jit(solution)/shard_map/stack_fwd/pallas_call | solution.py:300
  52.7 180.5 %stack_back.1 = (f32[16,768]{1,0:T(8,128)}, f32[16,384]{1,0:T(8,128)}, f32[16,128]{1,0:T(8,128)}, f32[48,2304]{1,0:T(8,128)}, f32[48,768]{1,0:T(8,128)}, /*index...) custom-call(s32[2,1,512]{2,1,0:T(1,128)} %seg.3, ...), custom_call_target="tpu_custom_call" | custom-call | tf_op jit(solution)/shard_map/stack_back/pallas_call | solution.py:1121
  233.2 4.5 %finish.1 = (f32[2,4,384]{2,1,0:T(4,128)}, f32[2,4]{1,0:T(2,128)}, f32[2,512,384]{2,1,0:T(8,128)}, f32[48,2304]{1,0:T(8,128)}, f32[48,768]{1,0:T(8,128)}, /*inde...) custom-call(f32[16,768]{1,0:T(8,128)} %get-tuple-element.65.vec, ...), custom_call_target="tpu_custom_call" | custom-call | tf_op jit(solution)/shard_map/finish/pallas_call | solution.py:1183
